TPU v7x, 256 devices: a whole 4x4x8 slice. The times are simulated.
256 devices in a mesh: dp: 16 (over x, y), mp: 16 (over z, core).
Axes of the slice: x: 4, y: 4, z: 8, core: 2. Of those that a mesh axis runs over, the one named last changes fastest.
Arguments:
- train_acts: bfloat16 [2048, 4096], P('dp', 'mp'), may hold values from -6 to 6
- train_grads: bfloat16 [2048, 7168], P('dp', 'mp'), may hold values from -0.75 to 0.75
- query_acts: bfloat16 [1024, 4096], P('dp', 'mp'), may hold values from -6 to 6
- query_grads: bfloat16 [1024, 7168], P('dp', 'mp'), may hold values from -0.75 to 0.75
- basis_in: bfloat16 [4096, 4096], P('mp'), may hold values from -0.125 to 0.125
- basis_out: bfloat16 [7168, 7168], P('mp'), may hold values from -0.09375 to 0.09375
- eigvals: bfloat16 [4096, 7168], P(None, 'mp'), may hold values from 0.25 to 4
Outputs:
- scores: float32 [16, 32], P(None, 'dp')
- energies: float32 [32], P('dp')
All inputs are finite; a program needn't handle non-finite values.
Results may differ from a plain program's by a relative error of at most 0.0048.
Values may be sent and summed in bfloat16 or wider, within the bound.
A program may use at most 128 MiB of HBM per device.

v0:
```python
import math

import jax
import jax.numpy as jnp
from jax import lax
from jax.sharding import PartitionSpec as P

D = 4096
H = 7168
SEQ = 64


damping = 0.1


def pair_scores(query_a, query_g, scaled):
    applied = jnp.einsum("it,nij->ntj", query_a, scaled, preferred_element_type=jnp.float32)
    per_token = jnp.sum(applied * jnp.transpose(query_g).astype(jnp.float32)[None], axis=2)
    grouped = jnp.sum(per_token.reshape(per_token.shape[0], -1, SEQ), axis=2)
    return jnp.transpose(grouped)


def on_device(train_acts, train_grads, query_acts, query_grads, basis_in, basis_out, eigvals):
    train_rows = train_acts.shape[0]
    train_seqs = train_rows // SEQ
    acts = jnp.concatenate([train_acts, query_acts], axis=0)
    grads = jnp.concatenate([train_grads, query_grads], axis=0)
    columns = basis_in
    rot_acts = lax.psum(
        jnp.einsum("fc,rf->cr", columns, acts, preferred_element_type=jnp.float32), "mp"
    ).astype(jnp.bfloat16)
    columns = basis_out
    rot_grads = lax.psum_scatter(
        jnp.einsum("fc,rf->cr", columns, grads, preferred_element_type=jnp.float32),
        "mp",
        scatter_dimension=0,
        tiled=True,
    ).astype(jnp.bfloat16)
    train_a = rot_acts[:, :train_rows].reshape(rot_acts.shape[0], train_seqs, SEQ)
    train_g = rot_grads[:, :train_rows].reshape(rot_grads.shape[0], train_seqs, SEQ)
    query_a = rot_acts[:, train_rows:]
    query_g = rot_grads[:, train_rows:]
    train_outer = jnp.einsum("isk,jsk->sij", train_a, train_g, preferred_element_type=jnp.float32)
    shifted = eigvals.astype(jnp.float32) + damping
    scaled = (train_outer / shifted).astype(jnp.bfloat16)
    energy_part = jnp.sum(train_outer * train_outer, axis=(1, 2))
    all_query_a, all_query_g = (
        lax.all_gather(query_a, "dp", axis=1, tiled=True),
        lax.all_gather(query_g, "dp", axis=1, tiled=True),
    )
    partial_value = pair_scores(all_query_a, all_query_g, scaled)
    total_scores, total_energy = lax.psum((partial_value, energy_part), "mp")
    scores = total_scores * (1.0 / math.sqrt(D * H))
    energies = total_energy / (D * H)
    return (scores, energies)


def solution(mesh):
    return jax.shard_map(
        on_device,
        mesh=mesh,
        in_specs=(
            P("dp", "mp"),
            P("dp", "mp"),
            P("dp", "mp"),
            P("dp", "mp"),
            P("mp", None),
            P("mp", None),
            P(None, "mp"),
        ),
        out_specs=(P(None, "dp"), P("dp")),
        check_vma=False,
    )
```

profile of v0, /device:TPU:1, one launch (start us, length us, event | category | flops | bytes accessed | tf_op | source)
XLA Modules:
  0.0 231.1 jit_solution(8527302216711309)
XLA Ops:
  8.1 1.1 copy.13
  9.2 6.9 %convolution_bitcast_fusion = f32[7168,192]{0,1:T(8,128)} fusion(bf16[448,7168]{1,0:T(8,128)(2,1)} %param.12, bf16[64,448]{0,1:T(8,128)(2,1)S(1)} %copy.13, bf16[128,448]{0,1:T(8,128)(2,1)} %param.8), kind=kOutput, calls=%fused_computation.2 | convolution fusion | flops 1233469440 | bytes 12099584 | tf_op jit(solution)/shard_map/fc,rf->cr/dot_general | solution.py:34
  16.1 7.6 %copy.15 = f32[7168,192]{1,0:T(8,128)} copy(f32[7168,192]{0,1:T(8,128)} %convolution_bitcast_fusion) | data formatting | bytes 11010048
  23.7 0.0 all-gather.2.cloned.1.call-start
  23.8 0.7 copy-done.3
  24.5 2.3 convolution_bitcast_fusion.1
  26.8 78.1 %all-reduce.2 = bf16[4096,192]{0,1:T(8,128)(2,1)S(1)} all-reduce(f32[4096,192]{0,1:T(8,128)} %convolution_bitcast_fusion.1), channel_id=1, replica_groups=mesh['dp'=16,'mp'=16] {'mp'}, use_global_device_ids=true, to_apply=%region_0.0 | all-reduce | flops 786432 | bytes 4718592 | tf_op jit(solution)/shard_map/psum | solution.py:29
  104.9 0.9 slice.18
  105.8 6.0 %convert_add_fusion = f32[4096,448]{0,1:T(8,128)} fusion(bf16[4096,448]{0,1:T(8,128)(2,1)} %param.13), kind=kLoop, calls=%fused_computation.5 | loop fusion | flops 3670016 | bytes 11010048 | tf_op jit(solution)/shard_map/add | solution.py:44
  111.9 1.0 slice.17
  112.9 0.1 copy.17
  113.1 1.0 slice.19
  114.0 0.1 copy.18
  114.1 22.9 %all_gather.7 = bf16[448,1024]{0,1:T(8,128)(2,1)S(1)} all-gather(bf16[448,64]{0,1:T(8,128)(2,1)S(1)} %copy.18), channel_id=1, replica_groups=mesh['dp'=16,'mp'=16] {'dp'}, dimensions={1}, use_global_device_ids=true | all-gather | bytes 974848 | tf_op jit(solution)/shard_map/all_gather | solution.py:49
  137.0 0.3 convert_bitcast_fusion
  137.3 1.8 copy.14
  139.1 7.4 %multiply_reduce_fusion = (f32[2]{0:T(128)S(1)}, f32[2,4096,448]{1,2,0:T(8,128)}) fusion(bf16[4096,2,64]{0,2,1:T(8,128)(2,1)S(1)} %bitcast.23, bf16[448,2,64]{0,2,1:T(8,128)(2,1)S(1)} %bitcast.24), kind=kOutput, calls=%fused_computation | convolution fusion | flops 477102080 | bytes 15843336 | tf_op jit(solution)/shard_map/isk,jsk->sij/dot_general | solution.py:43
  146.4 36.9 %all-gather.2.cloned.1.call-done = bf16[4096,1024]{0,1:T(8,128)(2,1)} async-done(((bf16[4096,64]{0,1:T(8,128)(2,1)}), bf16[4096,1024]{0,1:T(8,128)(2,1)}) %all-gather.2.cloned.1.call-update) | async-done | bytes 8388624 | tf_op jit(solution)/shard_map/all_gather | solution.py:48
  183.3 15.0 %fusion.2 = f32[2,1024]{1,0:T(2,128)S(1)} fusion(bf16[4096,1024]{0,1:T(8,128)(2,1)} %all-gather.2.cloned.1.call-done, f32[2,4096,448]{1,2,0:T(8,128)} %get-tuple-element.5, f32[4096,448]{0,1:T(8,128)} %convert_add_fusion, f32[1024,448]{0,1:T(8,128)} %copy.14), kind=kOutput, calls=%fused_computation.8 | convolution fusion | flops 7525365760 | bytes 32251904 | tf_op jit(solution)/shard_map/it,nij->ntj/dot_general | solution.py:17
  198.3 0.1 reshape.17
  198.3 0.1 reduce_sum.28
  198.4 24.1 %all-reduce = (f32[16,2]{0,1:T(2,128)S(1)}, f32[2]{0:T(128)S(1)}) all-reduce(f32[16,2]{0,1:T(2,128)S(1)} %bitcast.25, f32[2]{0:T(128)S(1)} %get-tuple-element.4), channel_id=1, replica_groups=mesh['dp'=16,'mp'=16] {'mp'}, use_global_device_ids=true, to_apply=%region_4.0 | all-reduce | flops 34 | bytes 272 | tf_op jit(solution)/shard_map/psum | solution.py:52
  222.6 0.6 broadcast_multiply_fusion
  223.1 0.5 broadcast_multiply_fusion.1
  (15 shorter events, 0.1 us)
Async XLA Ops:
  8.0 15.8 %copy-start = (bf16[256,4096]{1,0:T(8,128)(2,1)S(1)}, bf16[256,4096]{1,0:T(8,128)(2,1)}, u32[]{:S(2)}) copy-start(bf16[256,4096]{1,0:T(8,128)(2,1)} %param.11) | copy-start | bytes 6291460
  8.0 103.9 %reduce-scatter.4.cloned.1.call-start = ((), (), s32[]{:S(2)}) async-start(), calls=%async_computation.2 | async-start | bytes 7798784
  23.7 0.8 copy-start.3
  23.7 0.8 copy-start.4
  23.7 159.6 %all-gather.2.cloned.1.call-start = ((), (), s32[]{:S(2)}) async-start(), calls=%async_computation.1 | async-start | bytes 8912896 | tf_op jit(solution)/shard_map/all_gather | solution.py:48
  104.9 7.0 %copy-start.2 = (bf16[4096,192]{0,1:T(8,128)(2,1)}, bf16[4096,192]{0,1:T(8,128)(2,1)S(1)}, u32[]{:S(2)}) copy-start(bf16[4096,192]{0,1:T(8,128)(2,1)S(1)} %all-reduce.2) | copy-start | bytes 4718596
  111.9 27.2 %slice-start = ((bf16[4096,192]{0,1:T(8,128)(2,1)}), bf16[4096,128]{0,1:T(8,128)(2,1)S(1)}, s32[]{:S(2)}) async-start(bf16[4096,192]{0,1:T(8,128)(2,1)} %copy-done.2), calls=%async_computation.3 | async-start | bytes 2097152 | tf_op jit(solution)/shard_map/slice | solution.py:39
  183.3 40.4 %copy-start.1 = (bf16[256,4096]{1,0:T(8,128)(2,1)S(1)}, bf16[256,4096]{1,0:T(8,128)(2,1)}, u32[]{:S(2)}) copy-start(bf16[256,4096]{1,0:T(8,128)(2,1)} %param.11) | copy-start | bytes 6291460
Sparse Core Ops, SparseCore 0:
  23.8 87.5 reduce-scatter.3
Sparse Core Ops, SparseCore 1:
  105.9 77.3 all-gather.1
where the time goes:
time: 233 us; the launch traced here: 231 us
  blocking collectives  125 us (54%)
  waiting for transfers between devices  36.9 us (16%)
  matrix products  31.5 us (14%)
  between operations  15.6 us (7%)
  local copies, waits for them, and re-layouts  14.5 us (6%)
  other arithmetic  7.49 us (3%)
    psum x1, blocking collectives, on_device(): lax.psum(jnp.einsum('fc,rf->cr', columns, acts, preferred_element_type=jn...  78.1 us
    all_gather x1, waiting for transfers between devices, on_device(): lax.all_gather(query_a, 'dp', axis=1, tiled=True)  36.9 us
    psum x1, blocking collectives, on_device(): total_scores, total_energy = lax.psum((partial_value, energy_part), 'mp')  24.1 us
    all_gather x1, blocking collectives, on_device(): lax.all_gather(query_g, 'dp', axis=1, tiled=True)  22.9 us
    dot_general x1, matrix products, pair_scores(): jnp.einsum('it,nij->ntj', query_a, scaled, preferred_element_type=jnp.flo...  15 us
    unnamed x14, local copies, waits for them, and re-layouts  9.7 us
    dot_general x1, matrix products, on_device(): jnp.einsum('isk,jsk->sij', train_a, train_g, preferred_element_type=jnp.f...  7.35 us
    dot_general x1, matrix products, on_device(): jnp.einsum('fc,rf->cr', columns, grads, preferred_element_type=jnp.float32)  6.88 us
  transfers between devices with their start and end apart: 2, of which 1 were waited for; matrix products, arithmetic and copies ran while one was open for 9% of the time, Pallas kernels for 0%

commit v1 on v0

v1 whole, which is shorter than its diff:
```python
import math

import jax
import jax.numpy as jnp
from jax import lax
from jax.experimental import pallas as pl
from jax.experimental.pallas import tpu as pltpu
from jax.sharding import PartitionSpec as P

D = 4096
H = 7168
SEQ = 64
DAMPING = 0.1
IB = 256
JB = 896
FG = 448
FA = 256
NQ = 32
NT = 64
NR = NQ + NT
HALF = NR // 2
BF = jnp.bfloat16
F32 = jnp.float32
MESH = pl.DeviceIdType.MESH


def dot(a, b):
    return jnp.dot(a, b, preferred_element_type=F32)


def kernel(
    ta_hbm, qa_hbm, tgt_hbm, qg_hbm, bi_hbm, bo_hbm, eig_hbm, out_ref,
    B, XG, TGT, TGS, PART, SIBS, SIBR, GPS, GSS, GPR, GSR, G96, QGS,
    ACT, BI, EIG, INV, APS, ASS, APR, ASR, RA, QAS, QAF, S, ACC, ENE, MSG, R1, R2, X2,
    load_sem, b_sem, swap_send, swap_recv, sib_send, sib_recv,
    gp_send, gp_recv, gs_send, gs_recv, ap_send, ap_recv, as_send, as_recv,
    xa_send, xa_recv, xg_send, xg_recv, qg_send, qg_recv, za_send, za_recv, qa_send, qa_recv,
    r1_send, r1_recv, r2_send, r2_recv,
):
    d = lax.axis_index("dp")
    m = lax.axis_index("mp")
    z = m // 2
    c = m % 2
    s = 1 - 2 * c
    o = 1 - c
    su = 4 - 3 * c
    sv = 1 + 3 * c
    u = (d // su) % 4
    v = (d // sv) % 4
    sib = (d, 2 * z + o)

    def zdev(delta):
        return (d, 2 * ((z + delta + 8) % 8) + c)

    def slot_at(du, dv):
        return ((u + du + 4) % 4) * su + ((v + dv + 4) % 4) * sv

    def dpdev(du, dv):
        return (slot_at(du, dv), m)

    def remote(src, dst, send, recv, dev):
        return pltpu.make_async_remote_copy(
            src_ref=src, dst_ref=dst, send_sem=send, recv_sem=recv, device_id=dev, device_id_type=MESH
        )

    sends = []

    def push(src, dst, send, recv, dev):
        copy = remote(src, dst, send, recv, dev)
        copy.start()
        sends.append(copy)

    def arrived(dst, recv):
        remote(dst, dst, recv, recv, sib).wait_recv()

    def zoff(k):
        h = (k + 1) // 2
        return (4 - h) * (2 * (k % 2) - 1)

    def target(k):
        return (z + zoff(k) + 8) % 8

    loads = []

    def load(src, dst, sem):
        copy = pltpu.make_async_copy(src, dst, sem)
        copy.start()
        loads.append(copy)
        return copy

    own_cols = pl.ds(pl.multiple_of(c * FA, FA), FA)
    i_cols = pl.ds(pl.multiple_of(d * IB, IB), IB)

    def rows(cls, size):
        return pl.ds(pl.multiple_of(cls * size, size), size)

    l_tgt = load(tgt_hbm, TGT, load_sem.at[0])
    l_qg0 = load(qg_hbm.at[rows(c, NQ)], XG.at[pl.ds(0, NQ)], load_sem.at[1])
    l_qg1 = load(qg_hbm.at[rows(o, NQ)], XG.at[pl.ds(NR, NQ)], load_sem.at[2])
    b_loads = []
    for k in range(8):
        col = pl.multiple_of(target(k) * JB, 128)
        b_loads.append(load(bo_hbm.at[:, pl.ds(col, JB)], B.at[k], b_sem.at[k]))
    l_ta = load(ta_hbm.at[rows(c, NT)], ACT.at[d, pl.ds(NQ, NT), own_cols], load_sem.at[3])
    l_qa = load(qa_hbm.at[rows(c, NQ)], ACT.at[d, pl.ds(0, NQ), own_cols], load_sem.at[4])
    l_bi = load(bi_hbm.at[:, i_cols], BI.at[own_cols], load_sem.at[5])
    eig_rows = pl.ds(pl.multiple_of(c * FG, FG), FG)
    l_eig = load(eig_hbm.at[:, i_cols], EIG.at[eig_rows], load_sem.at[6])

    barrier = pltpu.get_barrier_semaphore()
    for k in range(1, 16):
        pl.semaphore_signal(barrier, inc=1, device_id=((d + k) % 16, m), device_id_type=MESH)
        pl.semaphore_signal(barrier, inc=1, device_id=(d, (m + k) % 16), device_id_type=MESH)
    pl.semaphore_wait(barrier, 30)

    push(ta_hbm.at[rows(o, NT)], ACT.at[d, pl.ds(NQ, NT), own_cols], swap_send.at[0], swap_recv.at[0], sib)
    push(qa_hbm.at[rows(o, NQ)], ACT.at[d, pl.ds(0, NQ), own_cols], swap_send.at[1], swap_recv.at[1], sib)
    push(bi_hbm.at[:, i_cols], BI.at[own_cols], swap_send.at[2], swap_recv.at[2], sib)
    push(eig_hbm.at[:, i_cols], EIG.at[eig_rows], swap_send.at[3], swap_recv.at[3], sib)
    sib_cols = pl.ds(pl.multiple_of(o * FA, FA), FA)

    l_tgt.wait()
    TGS[...] = jnp.transpose(TGT[...].astype(F32)).astype(BF)
    XG[pl.ds(NQ, NT), :] = TGS[rows(c, NT), :]
    XG[pl.ds(NR + NQ, NT), :] = TGS[rows(o, NT), :]
    l_qg0.wait()
    l_qg1.wait()

    def g_partial(k):
        b_loads[k].wait()
        part = dot(XG[...], B[k])
        PART[k] = part[:NR]
        SIBS[k] = part[NR:]
        push(SIBS.at[k], SIBR.at[k], sib_send.at[k], sib_recv.at[k], sib)

    def gather_stages(buf, send, recv):
        count = [0]

        def go(slot, dev):
            push(buf.at[slot], buf.at[slot], send.at[count[0]], recv.at[slot], dev)
            count[0] += 1

        def got(slot):
            arrived(buf.at[slot], recv.at[slot])

        def along_v(du):
            go(slot_at(du, 0), dpdev(0, 1))
            go(slot_at(du, 0), dpdev(0, -1))

        def stage_a():
            go(slot_at(0, 0), dpdev(s, 0))
            go(slot_at(0, 0), dpdev(-s, 0))
            along_v(0)
            return []

        def stage_b():
            got(slot_at(-s, 0))
            go(slot_at(-s, 0), dpdev(s, 0))
            along_v(-s)
            got(slot_at(s, 0))
            along_v(s)
            return [slot_at(-s, 0), slot_at(s, 0)]

        def stage_c():
            got(slot_at(0, -1))
            go(slot_at(0, -1), dpdev(0, 1))
            got(slot_at(0, 1))
            got(slot_at(2, 0))
            along_v(2)
            return [slot_at(0, -1), slot_at(0, 1), slot_at(2, 0)]

        def stage_d():
            done = []
            for du in (-s, s):
                got(slot_at(du, 1))
                go(slot_at(du, 1), dpdev(0, -1))
                got(slot_at(du, -1))
                done += [slot_at(du, 1), slot_at(du, -1)]
            return done

        def stage_e():
            got(slot_at(2, -1))
            go(slot_at(2, -1), dpdev(0, 1))
            got(slot_at(2, 1))
            got(slot_at(0, 2))
            return [slot_at(2, -1), slot_at(2, 1), slot_at(0, 2)]

        def stage_f():
            done = []
            for du in (-s, s, 2):
                got(slot_at(du, 2))
                done.append(slot_at(du, 2))
            return done

        return [stage_a, stage_b, stage_c, stage_d, stage_e, stage_f]

    xa = gather_stages(ACT, xa_send, xa_recv)
    xg = gather_stages(G96, xg_send, xg_recv)

    def g_query_to_sibling(slots):
        for slot in slots:
            push(G96.at[slot, pl.ds(0, NQ)], QGS.at[slot], qg_send.at[slot], qg_recv.at[slot], sib)

    def g_own(k, h):
        part = pl.ds(h * HALF, HALF)
        return PART[k, part, :] + SIBR[k, part, :]

    def g_ring(step):
        kp = 0 if step == 0 else 2 * step - 1 + c
        arrived(SIBR.at[kp], sib_recv.at[kp])
        if step < 3:
            ks = 2 * (step + 1) - c
            arrived(SIBR.at[ks], sib_recv.at[ks])
        for h in range(2):
            part = pl.ds(h * HALF, HALF)
            total = g_own(kp, h)
            if step > 0:
                arrived(GPR.at[step - 1, part], gp_recv.at[step - 1, h])
                total = total + GPR[step - 1, part, :].astype(F32)
            GPS[step, part, :] = total.astype(BF)
            push(GPS.at[step, part], GPR.at[step, part], gp_send.at[step, h], gp_recv.at[step, h], zdev(s))
            if step < 3:
                total = g_own(ks, h)
                if step > 0:
                    arrived(GSR.at[step - 1, part], gs_recv.at[step - 1, h])
                    total = total + GSR[step - 1, part, :].astype(F32)
                GSS[step, part, :] = total.astype(BF)
                push(GSS.at[step, part], GSR.at[step, part], gs_send.at[step, h], gs_recv.at[step, h], zdev(-s))

    def g_final():
        arrived(SIBR.at[7], sib_recv.at[7])
        for h in range(2):
            part = pl.ds(h * HALF, HALF)
            total = g_own(7, h)
            arrived(GSR.at[2, part], gs_recv.at[2, h])
            total = total + GSR[2, part, :].astype(F32)
            arrived(GPR.at[3, part], gp_recv.at[3, h])
            total = total + GPR[3, part, :].astype(F32)
            G96[d, part, :] = total.astype(BF)

    def a_own(delta, h):
        slot = 2 * ((z + delta + 8) % 8) + h
        return dot(ACT[slot], BI[...])

    def a_ring(step):
        for h in range(2):
            total = a_own(s * (4 - step), h)
            if step > 0:
                arrived(APR.at[step - 1, h], ap_recv.at[step - 1, h])
                total = total + APR[step - 1, h]
            APS[step, h] = total
            push(APS.at[step, h], APR.at[step, h], ap_send.at[step, h], ap_recv.at[step, h], zdev(s))
            if step < 3:
                total = a_own(-s * (3 - step), h)
                if step > 0:
                    arrived(ASR.at[step - 1, h], as_recv.at[step - 1, h])
                    total = total + ASR[step - 1, h]
                ASS[step, h] = total
                push(ASS.at[step, h], ASR.at[step, h], as_send.at[step, h], as_recv.at[step, h], zdev(-s))

    def a_final():
        for h in range(2):
            total = a_own(0, h)
            arrived(ASR.at[2, h], as_recv.at[2, h])
            total = total + ASR[2, h]
            arrived(APR.at[3, h], ap_recv.at[3, h])
            total = total + APR[3, h]
            RA[2 * z + h] = total.astype(BF)

    kind_rows = (pl.ds(0, NQ), pl.ds(NQ, NT))

    def za_ref(delta, kind):
        block = (z + delta + 8) % 8
        return RA.at[pl.ds(2 * block, 2), kind_rows[kind]]

    def za_index(delta):
        return (z + delta + 8) % 8

    za_count = [0]

    def za_go(delta, kind, dev):
        ref = za_ref(delta, kind)
        push(ref, ref, za_send.at[za_count[0]], za_recv.at[za_index(delta), kind], dev)
        za_count[0] += 1

    def za_got(delta, kind):
        arrived(za_ref(delta, kind), za_recv.at[za_index(delta), kind])

    def za_share(delta):
        block = za_index(delta)
        push(za_ref(delta, 0), QAS.at[pl.ds(2 * block, 2)], qa_send.at[block], qa_recv.at[block], sib)

    g_partial(0)
    g_partial(1)
    g_partial(2)
    g_ring(0)
    l_ta.wait()
    l_qa.wait()
    arrived(ACT.at[d, pl.ds(NQ, NT), sib_cols], swap_recv.at[0])
    arrived(ACT.at[d, pl.ds(0, NQ), sib_cols], swap_recv.at[1])
    xa[0]()
    g_partial(3)
    g_partial(4)
    xa[1]()
    g_ring(1)
    g_partial(5)
    g_partial(6)
    g_partial(7)
    xa[2]()
    g_ring(2)
    xa[3]()
    l_bi.wait()
    l_eig.wait()
    sib_eig = pl.ds(pl.multiple_of(o * FG, FG), FG)
    arrived(BI.at[sib_cols], swap_recv.at[2])
    arrived(EIG.at[sib_eig], swap_recv.at[3])
    INV[...] = 1.0 / (EIG[...].astype(F32) + DAMPING)
    xa[4]()
    g_ring(3)
    xa[5]()
    a_ring(0)
    g_final()
    xg[0]()
    g_query_to_sibling([d])
    a_ring(1)
    g_query_to_sibling(xg[1]())
    a_ring(2)
    g_query_to_sibling(xg[2]())
    a_ring(3)
    g_query_to_sibling(xg[3]())
    a_final()
    za_go(0, 0, zdev(s))
    za_go(0, 0, zdev(-s))
    za_go(0, 1, zdev(s))
    za_go(0, 1, zdev(-s))
    za_share(0)
    g_query_to_sibling(xg[4]())
    for step in (1, 2, 3):
        for kind in range(2):
            za_got(-s * step, kind)
            za_go(-s * step, kind, zdev(s))
            za_got(s * step, kind)
            if step < 3:
                za_go(s * step, kind, zdev(-s))
            if kind == 0:
                za_share(-s * step)
                za_share(s * step)
    g_query_to_sibling(xg[5]())
    for kind in range(2):
        za_got(4, kind)
    za_share(4)
    for k in range(16):
        arrived(QGS.at[k], qg_recv.at[k])
    for k in range(8):
        arrived(QAS.at[pl.ds(2 * k, 2)], qa_recv.at[k])

    QAF[0] = RA[:, pl.ds(0, NQ), :].reshape(16 * NQ, IB).astype(F32)
    QAF[1] = QAS[...].reshape(16 * NQ, IB).astype(F32)

    def one_train(slot, carry):
        acts = RA[slot, pl.ds(NQ, NT), :]
        energy = jnp.zeros((8, 128), F32)
        for j in range(JB // 128):
            cols = pl.ds(j * 128, 128)
            outer = lax.dot_general(
                G96[slot, pl.ds(NQ, NT), cols], acts, (((0,), (0,)), ((), ())), preferred_element_type=F32
            )
            square = outer * outer
            energy = energy + jnp.sum((square[:, :128] + square[:, 128:]).reshape(16, 8, 128), axis=0)
            S[cols, :] = (outer * INV[cols, :]).astype(BF)
        ENE[slot] = energy
        total = jnp.zeros((16, 8, 128), F32)
        for cls in range(2):
            grads = G96[:, pl.ds(0, NQ), :] if cls == 0 else QGS[...]
            applied = dot(grads.reshape(16 * NQ, JB), S[...]) * QAF[cls]
            total = total + jnp.sum((applied[:, :128] + applied[:, 128:]).reshape(16, NQ // 8, 8, 128), axis=1)
        ACC[slot] = total.reshape(128, 128)
        return carry

    lax.fori_loop(0, 16, one_train, 0)

    ones = jnp.ones((8, 128), F32)
    for n in range(16):
        MSG[n, pl.ds(0, 8), :] = lax.dot_general(
            ones, ACC[n], (((1,), (1,)), ((), ())), precision=lax.Precision.HIGHEST, preferred_element_type=F32
        )
        MSG[n, pl.ds(8, 8), :] = ENE[n]
    R1[d] = MSG[d]
    for k in range(1, 16):
        peer = (d + k) % 16
        push(MSG.at[peer], R1.at[d], r1_send.at[k], r1_recv.at[d], (peer, m))
    for k in range(1, 16):
        peer = (d + k) % 16
        arrived(R1.at[peer], r1_recv.at[peer])
    X2[...] = jnp.sum(R1[...], axis=0)
    R2[m] = X2[...]
    for k in range(1, 16):
        peer = (m + k) % 16
        push(X2, R2.at[m], r2_send.at[k], r2_recv.at[m], (d, peer))
    for k in range(1, 16):
        peer = (m + k) % 16
        arrived(R2.at[peer], r2_recv.at[peer])
    for cls in range(2):
        total = R2[cls]
        for k in range(1, 8):
            total = total + R2[2 * k + cls]
        out_ref[cls] = total
    for copy in sends:
        copy.wait_send()


def on_device(train_acts, train_grads, query_acts, query_grads, basis_in, basis_out, eigvals):
    dma = pltpu.SemaphoreType.DMA
    vm = pltpu.VMEM
    sums = pl.pallas_call(
        kernel,
        out_shape=jax.ShapeDtypeStruct((2, 16, 128), F32),
        in_specs=[pl.BlockSpec(memory_space=pl.ANY)] * 7,
        out_specs=pl.BlockSpec(memory_space=pltpu.VMEM),
        scratch_shapes=[
            vm((8, FG, JB), BF),
            vm((2 * NR, FG), BF),
            vm((FG, 128), BF),
            vm((128, FG), BF),
            vm((8, NR, JB), F32),
            vm((8, NR, JB), F32),
            vm((8, NR, JB), F32),
            vm((4, NR, JB), BF),
            vm((3, NR, JB), BF),
            vm((4, NR, JB), BF),
            vm((3, NR, JB), BF),
            vm((16, NR, JB), BF),
            vm((16, NQ, JB), BF),
            vm((16, NR, 2 * FA), BF),
            vm((2 * FA, IB), BF),
            vm((JB, IB), BF),
            vm((JB, IB), F32),
            vm((4, 2, NR, IB), F32),
            vm((3, 2, NR, IB), F32),
            vm((4, 2, NR, IB), F32),
            vm((3, 2, NR, IB), F32),
            vm((16, NR, IB), BF),
            vm((16, NQ, IB), BF),
            vm((2, 16 * NQ, IB), F32),
            vm((JB, IB), BF),
            vm((16, 128, 128), F32),
            vm((16, 8, 128), F32),
            vm((16, 16, 128), F32),
            vm((16, 16, 128), F32),
            vm((16, 16, 128), F32),
            vm((16, 128), F32),
            dma((7,)), dma((8,)), dma((4,)), dma((4,)), dma((8,)), dma((8,)),
            dma((4, 2)), dma((4, 2)), dma((3, 2)), dma((3, 2)),
            dma((4, 2)), dma((4, 2)), dma((3, 2)), dma((3, 2)),
            dma((15,)), dma((16,)), dma((15,)), dma((16,)), dma((16,)), dma((16,)),
            dma((14,)), dma((8, 2)), dma((8,)), dma((8,)),
            dma((16,)), dma((16,)), dma((16,)), dma((16,)),
        ],
        compiler_params=pltpu.CompilerParams(
            collective_id=0, has_side_effects=True, vmem_limit_bytes=56 * 1024 * 1024
        ),
        cost_estimate=pl.CostEstimate(flops=10_000_000_000, bytes_accessed=8_000_000, transcendentals=0),
    )(train_acts, query_acts, train_grads.T, query_grads, basis_in, basis_out, eigvals.T)
    scores = jnp.sum(sums[:, 0, :].reshape(2, 16, 8), axis=2).T * (1.0 / math.sqrt(D * H))
    energies = jnp.sum(sums[:, 8:, :], axis=(1, 2)) / (D * H)
    return (scores, energies)


def solution(mesh):
    return jax.shard_map(
        on_device,
        mesh=mesh,
        in_specs=(
            P("dp", "mp"),
            P("dp", "mp"),
            P("dp", "mp"),
            P("dp", "mp"),
            P("mp", None),
            P("mp", None),
            P(None, "mp"),
        ),
        out_specs=(P(None, "dp"), P("dp")),
        check_vma=False,
    )
```

time: 233 us -> 101 us (0.43)
  blocking collectives: 125 us -> 0 us
  Pallas kernels: 0 us -> 97.8 us
  waiting for transfers between devices: 36.9 us -> 0 us
  matrix products: 31.5 us -> 0 us
  between operations: 15.6 us -> 0.64 us
  local copies, waits for them, and re-layouts: 14.5 us -> 0.79 us
  other arithmetic: 7.49 us -> 1.98 us
    psum x2 -> x0, blocking collectives: 102 us -> none  [the longest x1 78.1 us: on_device(): lax.psum(jnp.einsum('fc,rf->cr', columns, acts, preferred_element_type=jn...]
    pallas_call x0 -> x1, Pallas kernels: none -> 97.8 us  [on_device(): pl.pallas_call(kernel, out_shape=jax.ShapeDtypeStruct((2, 16, 128), F32),...]
    all_gather x1 -> x0, waiting for transfers between devices: 36.9 us -> none  [on_device(): lax.all_gather(query_a, 'dp', axis=1, tiled=True)]
    dot_general x4 -> x0, matrix products: 31.5 us -> none  [the longest x1 15 us: pair_scores(): jnp.einsum('it,nij->ntj', query_a, scaled, preferred_element_type=jnp.flo...]
    all_gather x1 -> x0, blocking collectives: 22.9 us -> none  [on_device(): lax.all_gather(query_g, 'dp', axis=1, tiled=True)]
    unnamed x14 -> x0, local copies, waits for them, and re-layouts: 9.7 us -> none
    add x1 -> x0, other arithmetic: 6.04 us -> none  [on_device(): shifted = eigvals.astype(jnp.float32) + damping]
  transfers between devices with their start and end apart: 2 -> 0, of which waited for: 1 -> 0; matrix products, arithmetic and copies ran while one was open for 9% -> 0% of each run, Pallas kernels for 0% -> 0%
where the time goes in v1:
time: 101 us
  Pallas kernels  97.8 us (97%)
  other arithmetic  1.98 us (2%)
    pallas_call x1, Pallas kernels, on_device(): pl.pallas_call(kernel, out_shape=jax.ShapeDtypeStruct((2, 16, 128), F32),...  97.8 us

profile of v1, /device:TPU:1, one launch (start us, length us, event | category | flops | bytes accessed | tf_op | source)
XLA Modules:
  0.0 101.2 jit_solution(7788290056138234550)
XLA Ops:
  0.6 97.8 %shard_map.86 = f32[2,16,128]{2,1,0:T(8,128)} custom-call(bf16[128,256]{1,0:T(8,128)(2,1)} %ta_hbm.1, bf16[64,256]{1,0:T(8,128)(2,1)} %qa_hbm.1, bf16[448,128]{1,0:T(8,128)(2,1)} %bitcast.5, bf16[64,448]{1,0:T(8,128)(2,1)} %qg_hbm.1, bf16[256,4096]{1,0:T(8,128)(2,1)} %bi_hbm.1, bf16[448,7168]{1,0:T(8,128)(2,1)} %bo_hbm.1, bf16[448,4096]{1,0:T(8,128)(2,1)} %bitcast.4), custom_call_target="tpu_custom_call" | custom-call | flops 10000000000 | bytes 8000000 | tf_op jit(solution)/shard_map/pallas_call | solution.py:415
  98.4 0.8 slice_reduce_fusion
  99.2 0.7 slice_reduce_fusion.1
  99.9 0.5 broadcast_multiply_fusion
  100.5 0.1 reshape_squeeze.3
  100.5 0.1 reduce_sum.18
  100.6 0.6 multiply_bitcast_fusion

commit v2 on v1

v2 whole, which is shorter than its diff:
```python
import math

import jax
import jax.numpy as jnp
from jax import lax
from jax.experimental import pallas as pl
from jax.experimental.pallas import tpu as pltpu
from jax.sharding import PartitionSpec as P

D = 4096
H = 7168
SEQ = 64
DAMPING = 0.1
IB = 256
JB = 896
FG = 448
FA = 256
NQ = 32
NT = 64
NR = NQ + NT
CUTS = 3
KINDS = NR // NQ
CUT = NR // CUTS
BF = jnp.bfloat16
F32 = jnp.float32
MESH = pl.DeviceIdType.MESH


def dot(a, b):
    return jnp.dot(a, b, preferred_element_type=F32)


def kernel(
    ta_hbm, qa_hbm, tgt_hbm, qg_hbm, bi_hbm, bo_hbm, eig_hbm, sc_ref, en_ref,
    B, XG, TGT, TGS, PART, SIBS, SIBR, GPS, GSS, GPR, GSR, G96, QGS,
    ACT, BI, EIG, INV, APART, APS, ASS, APR, ASR, RA, QAS, S, MSG, R1, R2, X2, R3,
    load_sem, b_sem, swap_send, swap_recv, sib_send, sib_recv,
    gp_send, gp_recv, gs_send, gs_recv, ap_send, ap_recv, as_send, as_recv,
    xa_send, xa_recv, xg_send, xg_recv, qg_send, qg_recv, za_send, za_recv, qa_send, qa_recv,
    r1_send, r1_recv, r2_send, r2_recv, r3_send, r3_recv,
):
    d = lax.axis_index("dp")
    m = lax.axis_index("mp")
    z = m // 2
    c = m % 2
    s = 1 - 2 * c
    o = 1 - c
    su = 4 - 3 * c
    sv = 1 + 3 * c
    u = (d // su) % 4
    v = (d // sv) % 4
    sib = (d, 2 * z + o)

    def zat(delta):
        return (z + delta + 8) % 8

    def zdev(delta):
        return (d, 2 * zat(delta) + c)

    def slot_at(du, dv):
        return ((u + du + 4) % 4) * su + ((v + dv + 4) % 4) * sv

    def dpdev(du, dv):
        return (slot_at(du, dv), m)

    def remote(src, dst, send, recv, dev):
        return pltpu.make_async_remote_copy(
            src_ref=src, dst_ref=dst, send_sem=send, recv_sem=recv, device_id=dev, device_id_type=MESH
        )

    sends = []

    def push(src, dst, send, recv, dev):
        copy = remote(src, dst, send, recv, dev)
        copy.start()
        sends.append(copy)

    def arrived(dst, recv):
        remote(dst, dst, recv, recv, sib).wait_recv()

    barrier = pltpu.get_barrier_semaphore()
    greeted = [sib, zdev(1), zdev(-1)] + [dpdev(k, 0) for k in (1, 2, 3)] + [dpdev(0, k) for k in (1, 2, 3)]
    for dev in greeted:
        pl.semaphore_signal(barrier, inc=1, device_id=dev, device_id_type=MESH)

    def zoff(k):
        h = (k + 1) // 2
        return (4 - h) * (2 * (k % 2) - 1)

    def target(k):
        return (z + zoff(k) + 8) % 8

    loads = []

    def load(src, dst, sem):
        copy = pltpu.make_async_copy(src, dst, sem)
        copy.start()
        loads.append(copy)
        return copy

    own_cols = pl.ds(pl.multiple_of(c * FA, FA), FA)
    i_cols = pl.ds(pl.multiple_of(d * IB, IB), IB)

    def rows(cls, size):
        return pl.ds(pl.multiple_of(cls * size, size), size)

    l_tgt = load(tgt_hbm, TGT, load_sem.at[0])
    l_qg0 = load(qg_hbm.at[rows(c, NQ)], XG.at[pl.ds(0, NQ)], load_sem.at[1])
    l_qg1 = load(qg_hbm.at[rows(o, NQ)], XG.at[pl.ds(NR, NQ)], load_sem.at[2])
    b_loads = []
    for k in range(8):
        col = pl.multiple_of(target(k) * JB, 128)
        b_loads.append(load(bo_hbm.at[:, pl.ds(col, JB)], B.at[k], b_sem.at[k]))
    l_ta = load(ta_hbm.at[rows(c, NT)], ACT.at[d, pl.ds(NQ, NT), own_cols], load_sem.at[3])
    l_qa = load(qa_hbm.at[rows(c, NQ)], ACT.at[d, pl.ds(0, NQ), own_cols], load_sem.at[4])
    l_bi = load(bi_hbm.at[:, i_cols], BI.at[own_cols], load_sem.at[5])
    eig_rows = pl.ds(pl.multiple_of(c * FG, FG), FG)
    l_eig = load(eig_hbm.at[:, i_cols], EIG.at[eig_rows], load_sem.at[6])

    sib_cols = pl.ds(pl.multiple_of(o * FA, FA), FA)

    l_tgt.wait()
    TGS[...] = jnp.transpose(TGT[...].astype(F32)).astype(BF)
    XG[pl.ds(NQ, NT), :] = TGS[rows(c, NT), :]
    XG[pl.ds(NR + NQ, NT), :] = TGS[rows(o, NT), :]
    l_qg0.wait()
    l_qg1.wait()

    def swap_inputs():
        push(ta_hbm.at[rows(o, NT)], ACT.at[d, pl.ds(NQ, NT), own_cols], swap_send.at[0], swap_recv.at[0], sib)
        push(qa_hbm.at[rows(o, NQ)], ACT.at[d, pl.ds(0, NQ), own_cols], swap_send.at[1], swap_recv.at[1], sib)
        push(bi_hbm.at[:, i_cols], BI.at[own_cols], swap_send.at[2], swap_recv.at[2], sib)
        push(eig_hbm.at[:, i_cols], EIG.at[eig_rows], swap_send.at[3], swap_recv.at[3], sib)

    def g_partial(k):
        b_loads[k].wait()
        part = dot(XG[...], B[k])
        PART[k] = part[:NR]
        SIBS[k] = part[NR:]

    def g_swap(k):
        push(SIBS.at[k], SIBR.at[k], sib_send.at[k], sib_recv.at[k], sib)

    def make_gather(buf, send, recv, landed):
        count = [0]

        def go(slot, dev):
            push(buf.at[slot], buf.at[slot], send.at[count[0]], recv.at[slot], dev)
            count[0] += 1

        def along_v(du):
            for dv in (1, 3, 2):
                go(slot_at(du, 0), dpdev(0, dv))

        def start():
            for du in (1, 3, 2):
                go(slot_at(0, 0), dpdev(du, 0))
            along_v(0)
            landed(slot_at(0, 0))

        def got(du, dv):
            slot = slot_at(du, dv)
            arrived(buf.at[slot], recv.at[slot])
            if dv == 0:
                along_v(du)
            landed(slot)

        return start, got

    def g_query_to_sibling(slot):
        push(G96.at[slot, pl.ds(0, NQ)], QGS.at[slot], qg_send.at[slot], qg_recv.at[slot], sib)

    xa_start, xa_got = make_gather(ACT, xa_send, xa_recv, lambda slot: None)
    xg_start, xg_got = make_gather(G96, xg_send, xg_recv, g_query_to_sibling)

    def g_own(k, h):
        part = pl.ds(h * CUT, CUT)
        return PART[k, part, :] + SIBR[k, part, :]

    def g_ring(step):
        kp = 0 if step == 0 else 2 * step - 1 + c
        arrived(SIBR.at[kp], sib_recv.at[kp])
        if step < 3:
            ks = 2 * (step + 1) - c
            arrived(SIBR.at[ks], sib_recv.at[ks])
        for h in range(CUTS):
            part = pl.ds(h * CUT, CUT)
            total = g_own(kp, h)
            if step > 0:
                arrived(GPR.at[step - 1, part], gp_recv.at[step - 1, h])
                total = total + GPR[step - 1, part, :].astype(F32)
            GPS[step, part, :] = total.astype(BF)
            push(GPS.at[step, part], GPR.at[step, part], gp_send.at[step, h], gp_recv.at[step, h], zdev(s))
            if step < 3:
                total = g_own(ks, h)
                if step > 0:
                    arrived(GSR.at[step - 1, part], gs_recv.at[step - 1, h])
                    total = total + GSR[step - 1, part, :].astype(F32)
                GSS[step, part, :] = total.astype(BF)
                push(GSS.at[step, part], GSR.at[step, part], gs_send.at[step, h], gs_recv.at[step, h], zdev(-s))

    def g_final():
        arrived(SIBR.at[7], sib_recv.at[7])
        for h in range(CUTS):
            part = pl.ds(h * CUT, CUT)
            total = g_own(7, h)
            arrived(GSR.at[2, part], gs_recv.at[2, h])
            total = total + GSR[2, part, :].astype(F32)
            arrived(GPR.at[3, part], gp_recv.at[3, h])
            total = total + GPR[3, part, :].astype(F32)
            G96[d, part, :] = total.astype(BF)

    kind_rows = tuple(pl.ds(k * NQ, NQ) for k in range(KINDS))

    def a_local(delta):
        block = zat(delta)
        both = dot(ACT[pl.ds(2 * block, 2)].reshape(2 * NR, 2 * FA), BI[...])
        APART[block] = both.reshape(2, NR, IB)

    def a_own(delta, kind):
        return APART[zat(delta), :, kind_rows[kind], :].reshape(2 * NQ, IB)

    def a_step(i):
        if i == 0:
            a_local(4 * s)
            a_local(-3 * s)
        for kind in range(KINDS):
            total = a_own(s * (4 - i), kind)
            if i > 0:
                arrived(APR.at[kind, i - 1], ap_recv.at[kind, i - 1])
                total = total + APR[kind, i - 1]
            APS[kind, i] = total
            push(APS.at[kind, i], APR.at[kind, i], ap_send.at[kind, i], ap_recv.at[kind, i], zdev(s))
            if i < 3:
                total = a_own(-s * (3 - i), kind)
                if i > 0:
                    arrived(ASR.at[kind, i - 1], as_recv.at[kind, i - 1])
                    total = total + ASR[kind, i - 1]
                ASS[kind, i] = total
                push(ASS.at[kind, i], ASR.at[kind, i], as_send.at[kind, i], as_recv.at[kind, i], zdev(-s))
        if i == 0:
            for delta in (3 * s, -2 * s, 2 * s, -s, s, 0):
                a_local(delta)

    def a_final(kind):
        total = a_own(0, kind)
        arrived(ASR.at[kind, 2], as_recv.at[kind, 2])
        total = total + ASR[kind, 2]
        arrived(APR.at[kind, 3], ap_recv.at[kind, 3])
        total = total + APR[kind, 3]
        RA[pl.ds(2 * z, 2), kind_rows[kind], :] = total.astype(BF).reshape(2, NQ, IB)

    def za_ref(delta, kind):
        block = (z + delta + 8) % 8
        return RA.at[pl.ds(2 * block, 2), kind_rows[kind]]

    def za_index(delta):
        return (z + delta + 8) % 8

    za_count = [0]

    def za_go(delta, kind, dev):
        ref = za_ref(delta, kind)
        push(ref, ref, za_send.at[za_count[0]], za_recv.at[za_index(delta), kind], dev)
        za_count[0] += 1

    def za_got(delta, kind):
        arrived(za_ref(delta, kind), za_recv.at[za_index(delta), kind])

    def za_share(delta):
        block = za_index(delta)
        push(za_ref(delta, 0), QAS.at[pl.ds(2 * block, 2)], qa_send.at[block], qa_recv.at[block], sib)

    def za_start(kind):
        za_go(0, kind, zdev(s))
        za_go(0, kind, zdev(-s))
        if kind == 0:
            za_share(0)

    def za_step(kind, step):
        za_got(-s * step, kind)
        if step < 4:
            za_go(-s * step, kind, zdev(s))
            za_got(s * step, kind)
            if step < 3:
                za_go(s * step, kind, zdev(-s))
        if kind == 0:
            za_share(-s * step)
            if step < 4:
                za_share(s * step)

    def outers(delta):
        def one(h, carry):
            slot = 2 * za_index(delta) + h
            acts = RA[slot, pl.ds(NQ, NT), :]
            energy = jnp.zeros((8, 128), F32)
            for j in range(JB // 128):
                cols = pl.ds(j * 128, 128)
                outer = lax.dot_general(
                    G96[slot, pl.ds(NQ, NT), cols], acts, (((0,), (0,)), ((), ())), preferred_element_type=F32
                )
                square = outer * outer
                energy = energy + jnp.sum((square[:, :128] + square[:, 128:]).reshape(16, 8, 128), axis=0)
                S[slot, cols, :] = (outer * INV[cols, :]).astype(BF)
            MSG[slot, pl.ds(16, 8), :] = energy
            return carry

        lax.fori_loop(0, 2, one, 0)

    def scores_of(slot):
        total = jnp.zeros((16, 8, 128), F32)
        for cls in range(2):
            grads = G96[:, pl.ds(0, NQ), :] if cls == 0 else QGS[...]
            acts = RA[:, pl.ds(0, NQ), :] if cls == 0 else QAS[...]
            applied = dot(grads.reshape(16 * NQ, JB), S[slot]) * acts.reshape(16 * NQ, IB).astype(F32)
            total = total + jnp.sum((applied[:, :128] + applied[:, 128:]).reshape(16, NQ // 8, 8, 128), axis=1)
        MSG[slot, pl.ds(0, 16), :] = jnp.sum(total, axis=1)

    def z_step(i):
        for kind in range(KINDS):
            za_step(kind, i)

    for k in (0, 1, 2):
        g_partial(k)
    pl.semaphore_wait(barrier, len(greeted))
    swap_inputs()
    for k in (0, 1, 2):
        g_swap(k)
    g_ring(0)
    l_ta.wait()
    l_qa.wait()
    arrived(ACT.at[d, pl.ds(NQ, NT), sib_cols], swap_recv.at[0])
    arrived(ACT.at[d, pl.ds(0, NQ), sib_cols], swap_recv.at[1])
    xa_start()
    for k in range(3, 8):
        g_partial(k)
        g_swap(k)
    g_ring(1)
    xa_got(1, 0)
    xa_got(3, 0)
    l_bi.wait()
    l_eig.wait()
    sib_eig = pl.ds(pl.multiple_of(o * FG, FG), FG)
    arrived(BI.at[sib_cols], swap_recv.at[2])
    arrived(EIG.at[sib_eig], swap_recv.at[3])
    INV[...] = 1.0 / (EIG[...].astype(F32) + DAMPING)
    xa_got(2, 0)
    g_ring(2)
    for du in (0, 1, 3, 2):
        if du == 2:
            g_ring(3)
        for dv in (1, 3, 2):
            xa_got(du, dv)
    a_step(0)
    g_final()
    xg_start()
    a_step(1)
    xg_got(1, 0)
    xg_got(3, 0)
    xg_got(2, 0)
    a_step(2)
    for dv in (1, 3, 2):
        xg_got(0, dv)
    a_step(3)
    for du in (1, 3):
        for dv in (1, 3, 2):
            xg_got(du, dv)
    for kind in range(KINDS):
        a_final(kind)
        za_start(kind)
    for dv in (1, 3, 2):
        xg_got(2, dv)
    outers(0)
    z_step(1)
    outers(1)
    outers(-1)
    z_step(2)
    outers(2)
    outers(-2)
    z_step(3)
    outers(3)
    outers(-3)
    z_step(4)
    outers(4)
    for k in range(16):
        arrived(QGS.at[k], qg_recv.at[k])
    for k in range(8):
        arrived(QAS.at[pl.ds(2 * k, 2)], qa_recv.at[k])

    def far(a):
        return (2 - a + 3 * (a // 2) + 2 * (a // 3) + 8) % 4

    def r1_copy(p):
        peer = slot_at(far(p // 4), far(p % 4))
        return remote(MSG.at[peer], R1.at[d], r1_send.at[p], r1_recv.at[d], (peer, m)), peer

    def one_train(p, carry):
        copy, peer = r1_copy(p)
        scores_of(peer)
        copy.start()
        return carry

    lax.fori_loop(0, 15, one_train, 0)
    scores_of(d)
    R1[d] = MSG[d]
    for k in range(1, 16):
        peer = (d + k) % 16
        arrived(R1.at[peer], r1_recv.at[peer])

    def over_lanes(x):
        return lax.dot_general(
            jnp.ones((8, 128), F32), x, (((1,), (1,)), ((), ())), precision=lax.Precision.HIGHEST,
            preferred_element_type=F32,
        )

    X2[...] = jnp.zeros((8, 128), F32)
    X2[:, pl.ds(0, 24)] = over_lanes(jnp.sum(R1[...], axis=0))
    R2[z] = X2[...]
    for delta in (4, 3, -3, 2, -2, 1, -1):
        push(X2, R2.at[z], r2_send.at[delta + 3], r2_recv.at[z], zdev(delta))
    for delta in (1, -1, 2, -2, 3, -3, 4):
        arrived(R2.at[zat(delta)], r2_recv.at[zat(delta)])
    R3[c] = jnp.sum(R2[...], axis=0)
    push(R3.at[c], R3.at[c], r3_send, r3_recv, sib)
    arrived(R3.at[o], r3_recv)
    for cls in range(2):
        sc_ref[pl.ds(cls, 1), :] = R3[cls, :1, :16]
        en_ref[:, pl.ds(cls, 1)] = jnp.sum(R3[cls, :1, 16:24], axis=1, keepdims=True)
    for copy in sends:
        copy.wait_send()
    for p in range(15):
        r1_copy(p)[0].wait_send()


def on_device(train_acts, train_grads, query_acts, query_grads, basis_in, basis_out, eigvals):
    dma = pltpu.SemaphoreType.DMA
    vm = pltpu.VMEM
    scores, energies = pl.pallas_call(
        kernel,
        out_shape=(jax.ShapeDtypeStruct((2, 16), F32), jax.ShapeDtypeStruct((1, 2), F32)),
        in_specs=[pl.BlockSpec(memory_space=pl.ANY)] * 7,
        out_specs=(pl.BlockSpec(memory_space=pltpu.VMEM),) * 2,
        scratch_shapes=[
            vm((8, FG, JB), BF),
            vm((2 * NR, FG), BF),
            vm((FG, 128), BF),
            vm((128, FG), BF),
            vm((8, NR, JB), F32),
            vm((8, NR, JB), F32),
            vm((8, NR, JB), F32),
            vm((4, NR, JB), BF),
            vm((3, NR, JB), BF),
            vm((4, NR, JB), BF),
            vm((3, NR, JB), BF),
            vm((16, NR, JB), BF),
            vm((16, NQ, JB), BF),
            vm((16, NR, 2 * FA), BF),
            vm((2 * FA, IB), BF),
            vm((JB, IB), BF),
            vm((JB, IB), F32),
            vm((8, 2, NR, IB), F32),
            vm((KINDS, 4, 2 * NQ, IB), F32),
            vm((KINDS, 3, 2 * NQ, IB), F32),
            vm((KINDS, 4, 2 * NQ, IB), F32),
            vm((KINDS, 3, 2 * NQ, IB), F32),
            vm((16, NR, IB), BF),
            vm((16, NQ, IB), BF),
            vm((16, JB, IB), BF),
            vm((16, 24, 128), F32),
            vm((16, 24, 128), F32),
            vm((8, 8, 128), F32),
            vm((8, 128), F32),
            vm((2, 8, 128), F32),
            dma((7,)), dma((8,)), dma((4,)), dma((4,)), dma((8,)), dma((8,)),
            dma((4, CUTS)), dma((4, CUTS)), dma((3, CUTS)), dma((3, CUTS)),
            dma((KINDS, 4)), dma((KINDS, 4)), dma((KINDS, 3)), dma((KINDS, 3)),
            dma((15,)), dma((16,)), dma((15,)), dma((16,)), dma((16,)), dma((16,)),
            dma((7 * KINDS,)), dma((8, KINDS)), dma((8,)), dma((8,)),
            dma((16,)), dma((16,)), dma((8,)), dma((8,)), dma, dma,
        ],
        compiler_params=pltpu.CompilerParams(
            collective_id=0, has_side_effects=True, vmem_limit_bytes=56 * 1024 * 1024
        ),
        cost_estimate=pl.CostEstimate(flops=10_000_000_000, bytes_accessed=8_000_000, transcendentals=0),
    )(train_acts, query_acts, train_grads.T, query_grads, basis_in, basis_out, eigvals.T)
    return (scores.T * (1.0 / math.sqrt(D * H)), energies.reshape(2) / (D * H))


def solution(mesh):
    return jax.shard_map(
        on_device,
        mesh=mesh,
        in_specs=(
            P("dp", "mp"),
            P("dp", "mp"),
            P("dp", "mp"),
            P("dp", "mp"),
            P("mp", None),
            P("mp", None),
            P(None, "mp"),
        ),
        out_specs=(P(None, "dp"), P("dp")),
        check_vma=False,
    )
```

time: 101 us -> 94.7 us (0.938)
  Pallas kernels: 97.8 us -> 91.2 us
    pallas_call x1, Pallas kernels: 97.8 us -> 91.2 us  [on_device(): pl.pallas_call(kernel, out_shape=(jax.ShapeDtypeStruct((2, 16), F32), jax...]
where the time goes in v2:
time: 94.7 us; the launch traced here: 94.2 us
  Pallas kernels  91.2 us (96%)
  other arithmetic  2.36 us (2%)
    pallas_call x1, Pallas kernels, on_device(): pl.pallas_call(kernel, out_shape=(jax.ShapeDtypeStruct((2, 16), F32), jax...  91.2 us

profile of v2, /device:TPU:1, one launch (start us, length us, event | category | flops | bytes accessed | tf_op | source)
XLA Modules:
  0.0 94.2 jit_solution(1366735807638888257)
XLA Ops:
  0.6 91.2 %shard_map.86 = (f32[2,16]{1,0:T(2,128)}, f32[1,2]{1,0:T(1,128)}) custom-call(bf16[128,256]{1,0:T(8,128)(2,1)} %ta_hbm.1, bf16[64,256]{1,0:T(8,128)(2,1)} %qa_hbm.1, bf16[448,128]{1,0:T(8,128)(2,1)} %bitcast.7, bf16[64,448]{1,0:T(8,128)(2,1)} %qg_hbm.1, bf16[256,4096]{1,0:T(8,128)(2,1)} %bi_hbm.1, bf16[448,7168]{1,0:T(8,128)(2,1)} %bo_hbm.1, ...), custom_call_target="tpu_custom_call" | custom-call | flops 10000000000 | bytes 8000000 | tf_op jit(solution)/shard_map/pallas_call | solution.py:438
  91.8 1.2 %multiply_bitcast_fusion = f32[16,2]{0,1:T(2,128)} fusion(f32[2,16]{1,0:T(2,128)} %get-tuple-element.4), kind=kLoop, calls=%fused_computation | loop fusion | flops 32 | bytes 256 | tf_op jit(solution)/shard_map/mul | solution.py:486
  93.0 1.1 %multiply_bitcast_fusion.1 = f32[2]{0:T(128)} fusion(f32[1,2]{1,0:T(1,128)} %get-tuple-element.5), kind=kLoop, calls=%fused_computation.1 | loop fusion | flops 2 | bytes 16 | tf_op jit(solution)/shard_map/div | solution.py:486

commit v3 on v2

--- a/solution.py
+++ b/solution.py
@@ -272,26 +272,34 @@
         push(za_ref(delta, 0), QAS.at[pl.ds(2 * block, 2)], qa_send.at[block], qa_recv.at[block], sib)
 
     def za_start(kind):
-        za_go(0, kind, zdev(s))
-        za_go(0, kind, zdev(-s))
+        for delta in (2, -2, 1, -1):
+            za_go(0, kind, zdev(delta))
         if kind == 0:
             za_share(0)
 
-    def za_step(kind, step):
-        za_got(-s * step, kind)
-        if step < 4:
-            za_go(-s * step, kind, zdev(s))
-            za_got(s * step, kind)
-            if step < 3:
-                za_go(s * step, kind, zdev(-s))
+    def za_far(kind):
+        za_got(-2 * s, kind)
+        za_go(-2 * s, kind, zdev(2 * s))
+        za_go(-2 * s, kind, zdev(s))
+        za_got(2 * s, kind)
+        za_go(2 * s, kind, zdev(-s))
         if kind == 0:
-            za_share(-s * step)
-            if step < 4:
-                za_share(s * step)
-
-    def outers(delta):
-        def one(h, carry):
-            slot = 2 * za_index(delta) + h
+            za_share(-2 * s)
+            za_share(2 * s)
+
+    def za_take(deltas, kind):
+        for delta in deltas:
+            za_got(delta, kind)
+            if kind == 0:
+                za_share(delta)
+
+    def nth_slot(p):
+        k = p // 2
+        return 2 * zat(((k + 1) // 2) * (2 * (k % 2) - 1)) + p % 2
+
+    def outers(first, last):
+        def one(p, carry):
+            slot = nth_slot(p)
             acts = RA[slot, pl.ds(NQ, NT), :]
             energy = jnp.zeros((8, 128), F32)
             for j in range(JB // 128):
@@ -305,7 +313,7 @@
             MSG[slot, pl.ds(16, 8), :] = energy
             return carry
 
-        lax.fori_loop(0, 2, one, 0)
+        lax.fori_loop(first, last, one, 0)
 
     def scores_of(slot):
         total = jnp.zeros((16, 8, 128), F32)
@@ -316,9 +324,25 @@
             total = total + jnp.sum((applied[:, :128] + applied[:, 128:]).reshape(16, NQ // 8, 8, 128), axis=1)
         MSG[slot, pl.ds(0, 16), :] = jnp.sum(total, axis=1)
 
-    def z_step(i):
-        for kind in range(KINDS):
-            za_step(kind, i)
+    def r1_copy(peer):
+        return remote(MSG.at[peer], R1.at[d], r1_send.at[peer], r1_recv.at[d], (peer, m))
+
+    def scores(first, last):
+        def one(p, carry):
+            slot = nth_slot(p)
+            scores_of(slot)
+
+            @pl.when(slot != d)
+            def _():
+                r1_copy(slot).start()
+
+            @pl.when(slot == d)
+            def _():
+                R1[d] = MSG[d]
+
+            return carry
+
+        lax.fori_loop(first, last, one, 0)
 
     for k in (0, 1, 2):
         g_partial(k)
@@ -326,12 +350,12 @@
     swap_inputs()
     for k in (0, 1, 2):
         g_swap(k)
-    g_ring(0)
     l_ta.wait()
     l_qa.wait()
     arrived(ACT.at[d, pl.ds(NQ, NT), sib_cols], swap_recv.at[0])
     arrived(ACT.at[d, pl.ds(0, NQ), sib_cols], swap_recv.at[1])
     xa_start()
+    g_ring(0)
     for k in range(3, 8):
         g_partial(k)
         g_swap(k)
@@ -362,47 +386,32 @@
     for dv in (1, 3, 2):
         xg_got(0, dv)
     a_step(3)
+    for kind in range(KINDS):
+        a_final(kind)
+        za_start(kind)
     for du in (1, 3):
         for dv in (1, 3, 2):
             xg_got(du, dv)
-    for kind in range(KINDS):
-        a_final(kind)
-        za_start(kind)
+    za_far(0)
     for dv in (1, 3, 2):
         xg_got(2, dv)
-    outers(0)
-    z_step(1)
-    outers(1)
-    outers(-1)
-    z_step(2)
-    outers(2)
-    outers(-2)
-    z_step(3)
-    outers(3)
-    outers(-3)
-    z_step(4)
-    outers(4)
+    outers(0, 2)
+    za_take((1, -1), 0)
+    za_far(1)
+    za_far(2)
+    for kind in (1, 2):
+        za_take((1, -1), kind)
+    outers(2, 10)
+    za_take((3, -3, 4), 0)
     for k in range(16):
         arrived(QGS.at[k], qg_recv.at[k])
     for k in range(8):
         arrived(QAS.at[pl.ds(2 * k, 2)], qa_recv.at[k])
-
-    def far(a):
-        return (2 - a + 3 * (a // 2) + 2 * (a // 3) + 8) % 4
-
-    def r1_copy(p):
-        peer = slot_at(far(p // 4), far(p % 4))
-        return remote(MSG.at[peer], R1.at[d], r1_send.at[p], r1_recv.at[d], (peer, m)), peer
-
-    def one_train(p, carry):
-        copy, peer = r1_copy(p)
-        scores_of(peer)
-        copy.start()
-        return carry
-
-    lax.fori_loop(0, 15, one_train, 0)
-    scores_of(d)
-    R1[d] = MSG[d]
+    scores(0, 10)
+    for kind in (1, 2):
+        za_take((3, -3, 4), kind)
+    outers(10, 16)
+    scores(10, 16)
     for k in range(1, 16):
         peer = (d + k) % 16
         arrived(R1.at[peer], r1_recv.at[peer])
@@ -428,8 +437,8 @@
         en_ref[:, pl.ds(cls, 1)] = jnp.sum(R3[cls, :1, 16:24], axis=1, keepdims=True)
     for copy in sends:
         copy.wait_send()
-    for p in range(15):
-        r1_copy(p)[0].wait_send()
+    for k in range(1, 16):
+        r1_copy((d + k) % 16).wait_send()
 
 
 def on_device(train_acts, train_grads, query_acts, query_grads, basis_in, basis_out, eigvals):

time: 94.7 us -> 92 us (0.971)
  Pallas kernels: 91.2 us -> 88.9 us
    pallas_call x1, Pallas kernels: 91.2 us -> 88.9 us  [on_device(): pl.pallas_call(kernel, out_shape=(jax.ShapeDtypeStruct((2, 16), F32), jax...]
where the time goes in v3:
time: 92 us; the launch traced here: 91.9 us
  Pallas kernels  88.9 us (97%)
  other arithmetic  2.36 us (3%)
    pallas_call x1, Pallas kernels, on_device(): pl.pallas_call(kernel, out_shape=(jax.ShapeDtypeStruct((2, 16), F32), jax...  88.9 us

profile of v3, /device:TPU:1, one launch (start us, length us, event | category | flops | bytes accessed | tf_op | source)
XLA Modules:
  0.0 91.9 jit_solution(16145071370419833430)
XLA Ops:
  0.6 88.9 %shard_map.86 = (f32[2,16]{1,0:T(2,128)}, f32[1,2]{1,0:T(1,128)}) custom-call(bf16[128,256]{1,0:T(8,128)(2,1)} %ta_hbm.1, bf16[64,256]{1,0:T(8,128)(2,1)} %qa_hbm.1, bf16[448,128]{1,0:T(8,128)(2,1)} %bitcast.7, bf16[64,448]{1,0:T(8,128)(2,1)} %qg_hbm.1, bf16[256,4096]{1,0:T(8,128)(2,1)} %bi_hbm.1, bf16[448,7168]{1,0:T(8,128)(2,1)} %bo_hbm.1, ...), custom_call_target="tpu_custom_call" | custom-call | flops 10000000000 | bytes 8000000 | tf_op jit(solution)/shard_map/pallas_call | solution.py:447
  89.6 1.2 %multiply_bitcast_fusion = f32[16,2]{0,1:T(2,128)} fusion(f32[2,16]{1,0:T(2,128)} %get-tuple-element.4), kind=kLoop, calls=%fused_computation | loop fusion | flops 32 | bytes 256 | tf_op jit(solution)/shard_map/mul | solution.py:495
  90.8 1.1 %multiply_bitcast_fusion.1 = f32[2]{0:T(128)} fusion(f32[1,2]{1,0:T(1,128)} %get-tuple-element.5), kind=kLoop, calls=%fused_computation.1 | loop fusion | flops 2 | bytes 16 | tf_op jit(solution)/shard_map/div | solution.py:495

commit v4 on v3

--- a/solution.py
+++ b/solution.py
@@ -238,9 +238,10 @@
                     total = total + ASR[kind, i - 1]
                 ASS[kind, i] = total
                 push(ASS.at[kind, i], ASR.at[kind, i], as_send.at[kind, i], as_recv.at[kind, i], zdev(-s))
-        if i == 0:
-            for delta in (3 * s, -2 * s, 2 * s, -s, s, 0):
-                a_local(delta)
+
+    def a_locals():
+        for delta in (3 * s, -2 * s, 2 * s, -s, s, 0):
+            a_local(delta)
 
     def a_final(kind):
         total = a_own(0, kind)
@@ -378,6 +379,7 @@
     a_step(0)
     g_final()
     xg_start()
+    a_locals()
     a_step(1)
     xg_got(1, 0)
     xg_got(3, 0)

time: 92 us -> 92.3 us (level)
  no operation moved by 1% of the time
where the time goes in v4:
time: 92.3 us; the launch traced here: 92.1 us
  Pallas kernels  89.1 us (97%)
  other arithmetic  2.36 us (3%)
    pallas_call x1, Pallas kernels, on_device(): pl.pallas_call(kernel, out_shape=(jax.ShapeDtypeStruct((2, 16), F32), jax...  89.1 us

profile of v4, /device:TPU:1, one launch (start us, length us, event | category | flops | bytes accessed | tf_op | source)
XLA Modules:
  0.0 92.1 jit_solution(10220237998975905043)
XLA Ops:
  0.6 89.1 %shard_map.86 = (f32[2,16]{1,0:T(2,128)}, f32[1,2]{1,0:T(1,128)}) custom-call(bf16[128,256]{1,0:T(8,128)(2,1)} %ta_hbm.1, bf16[64,256]{1,0:T(8,128)(2,1)} %qa_hbm.1, bf16[448,128]{1,0:T(8,128)(2,1)} %bitcast.7, bf16[64,448]{1,0:T(8,128)(2,1)} %qg_hbm.1, bf16[256,4096]{1,0:T(8,128)(2,1)} %bi_hbm.1, bf16[448,7168]{1,0:T(8,128)(2,1)} %bo_hbm.1, ...), custom_call_target="tpu_custom_call" | custom-call | flops 10000000000 | bytes 8000000 | tf_op jit(solution)/shard_map/pallas_call | solution.py:449
  89.8 1.2 %multiply_bitcast_fusion = f32[16,2]{0,1:T(2,128)} fusion(f32[2,16]{1,0:T(2,128)} %get-tuple-element.4), kind=kLoop, calls=%fused_computation | loop fusion | flops 32 | bytes 256 | tf_op jit(solution)/shard_map/mul | solution.py:497
  91.0 1.1 %multiply_bitcast_fusion.1 = f32[2]{0:T(128)} fusion(f32[1,2]{1,0:T(1,128)} %get-tuple-element.5), kind=kLoop, calls=%fused_computation.1 | loop fusion | flops 2 | bytes 16 | tf_op jit(solution)/shard_map/div | solution.py:497
